TPU v7x, 32 devices: a whole 2x2x4 slice. The times are simulated.
32 devices in a mesh: dp: 8 (over z, y), tensor: 4 (over x, core).
Axes of the slice: x: 2, y: 2, z: 4, core: 2. Of those that a mesh axis runs over, the one named last changes fastest.
Arguments:
- tokens: bfloat16 [24, 1024, 768], P('dp', 'tensor'), may hold values from -6 to 6
- cotangent: bfloat16 [24, 1024, 768], P('dp', 'tensor'), may hold values from -6 to 6
- lengths: int32 [24, 4], P('dp'), may hold values from 1 to 640, 1024 in all within a row
- row_counts: int32 [8], P('dp'), may hold values from 1 to 3, as said below
- attn_gain: float32 [768], replicated, may hold values from 0.25 to 1.75
- attn_shift: float32 [768], replicated, may hold values from -1.5 to 1.5
- qkv_weight: bfloat16 [3, 768, 768], P(None, None, 'tensor'), may hold values from -0.21875 to 0.21875
- qkv_bias: float32 [3, 768], P(None, 'tensor'), may hold values from -1.5 to 1.5
- out_weight: bfloat16 [768, 768], P('tensor'), may hold values from -1.25 to 1.25
- out_bias: float32 [768], replicated, may hold values from -1.5 to 1.5
- ffn_gain: float32 [768], replicated, may hold values from 0.25 to 1.75
- ffn_shift: float32 [768], replicated, may hold values from -1.5 to 1.5
- up_weight: bfloat16 [768, 3072], P(None, 'tensor'), may hold values from -0.21875 to 0.21875
- up_bias: float32 [3072], P('tensor'), may hold values from -1.5 to 1.5
- down_weight: bfloat16 [3072, 768], P('tensor'), may hold values from -0.109375 to 0.109375
- down_bias: float32 [768], replicated, may hold values from -1.5 to 1.5
- head_weight: bfloat16 [768, 70], replicated, may hold values from -0.3125 to 0.3125
- codon_freq: float32 [70], replicated, may hold values from 0.004 to 0.04
Outputs:
- mixed: bfloat16 [24, 1024, 768], P('dp', 'tensor')
- input_grad: bfloat16 [24, 1024, 768], P('dp', 'tensor')
- attn_gain_grad: float32 [768], replicated
- attn_shift_grad: float32 [768], replicated
- qkv_weight_grad: float32 [3, 768, 768], P(None, None, 'tensor')
- qkv_bias_grad: float32 [3, 768], P(None, 'tensor')
- out_weight_grad: float32 [768, 768], P('tensor')
- out_bias_grad: float32 [768], replicated
- ffn_gain_grad: float32 [768], replicated
- ffn_shift_grad: float32 [768], replicated
- up_weight_grad: float32 [768, 3072], P(None, 'tensor')
- up_bias_grad: float32 [3072], P('tensor')
- down_weight_grad: float32 [3072, 768], P('tensor')
- down_bias_grad: float32 [768], replicated
- codon_gap: float32 [8, 4, 70], P('dp', 'tensor')
Inputs may be any that keep to these rules, and one draw needn't show every extreme that they name: `row_counts`: the counts of the first j indices of dp sum to j * 2 or j * 2 + 1 for every j, and all counts to 2 times the number of dp indices; some index holds 3 live rows and some holds 1. Live rows come first in each index's slots.
All inputs are finite; a program needn't handle non-finite values.
Results may differ from a plain program's by a relative error of at most 0.018.
Values may be sent and summed in bfloat16 or wider, within the bound.
A program may use at most 128 MiB of HBM per device.

v0:
```python
import jax
import jax.numpy as jnp
from jax import lax
from jax.sharding import PartitionSpec as P

HEAD_DIM = 64


EPS = 1e-05
BASE = 10000.0


def prefix(value, axis, join, neutral):
    count, mine = (lax.axis_size(axis), lax.axis_index(axis))
    pieces = lax.all_gather(value, axis)
    total = jnp.full_like(value, 0) + jnp.asarray(neutral, value.dtype)

    def hop(position, total):
        longer = join(total, pieces[position])
        return jnp.where(position < mine, longer, total)

    return lax.fori_loop(0, count - 1, hop, total)


def shifted(value, axis, steps):
    count = lax.axis_size(axis)
    initial, last = (max(0, -steps), min(count, count - steps))
    return lax.ppermute(value, axis, [(source, source + steps) for source in range(initial, last)])


def norm_forward(value, gain, shift):
    average = jnp.mean(value, -1, keepdims=True)
    centred = value - average
    inv_std = lax.rsqrt(jnp.mean(centred * centred, -1, keepdims=True) + EPS)
    normed = centred * inv_std
    return (normed * gain + shift, normed, inv_std)


def norm_backward(incoming, normed, inv_std, gain):
    scaled = incoming * gain
    result = inv_std * (
        scaled
        - jnp.mean(scaled, -1, keepdims=True)
        - normed * jnp.mean(scaled * normed, -1, keepdims=True)
    )
    return (result, jnp.sum(incoming * normed, axis=(0, 1)), jnp.sum(incoming, axis=(0, 1)))


def gene_layout(lens, row_length):
    gene_ends = jnp.cumsum(lens, axis=1).astype(jnp.int32)
    starts = (gene_ends - lens).astype(jnp.int32)
    places = jnp.arange(row_length, dtype=jnp.int32)
    segment = jnp.sum((places[None, :, None] >= gene_ends[:, None, :]).astype(jnp.int32), axis=2)
    onehot = segment[:, :, None] == jnp.arange(lens.shape[1], dtype=jnp.int32)[None, None, :]
    gene_start = jnp.sum(jnp.where(onehot, starts[:, None, :], 0), axis=2)
    return (segment, places[None, :] - gene_start)


def rope_tables(position, half_dim):
    freqs = BASE ** (-jnp.arange(half_dim, dtype=jnp.float32) / half_dim)
    angles = position.astype(jnp.float32)[..., None] * freqs
    return (jnp.cos(angles), jnp.sin(angles))


def rotate_pairs(value, cosine, sine_table):
    half_dim = value.shape[-1] // 2
    front = value[..., :half_dim]
    back_half = value[..., half_dim:]
    cos_b = cosine[:, :, None, :]
    sin_b = sine_table[:, :, None, :]
    return jnp.concatenate(
        [front * cos_b - back_half * sin_b, back_half * cos_b + front * sin_b], axis=-1
    )


def masked_scores(queries, keys, segment):
    raw_scores = jnp.einsum(
        "qhe,khe->hqk", queries, keys, preferred_element_type=jnp.float32
    ) * HEAD_DIM ** (-0.5)
    same_gene = segment[:, None] == segment[None, :]
    return jnp.where(same_gene[None], raw_scores, -1e30)


def attend_row(parts):
    queries, keys, values, segment = parts
    scores = masked_scores(queries, keys, segment)
    row_max = jnp.max(scores, -1, keepdims=True)
    weights_raw = jnp.exp(scores - row_max)
    row_total = jnp.sum(weights_raw, -1, keepdims=True)
    probs = weights_raw / row_total
    outputs = jnp.einsum(
        "hqk,khe->qhe", probs.astype(jnp.bfloat16), values, preferred_element_type=jnp.float32
    )
    return (outputs, row_max + jnp.log(row_total))


def attend_back(parts):
    queries, keys, values, segment, log_total, grad_head = parts
    probs = jnp.exp(masked_scores(queries, keys, segment) - log_total)
    grad_probs = jnp.einsum("qhe,khe->hqk", grad_head, values, preferred_element_type=jnp.float32)
    row_dot = jnp.sum(probs * grad_probs, -1, keepdims=True)
    grad_scores = (probs * (grad_probs - row_dot)).astype(jnp.bfloat16)
    grad_queries = jnp.einsum(
        "hqk,khe->qhe", grad_scores, keys, preferred_element_type=jnp.float32
    ) * HEAD_DIM ** (-0.5)
    grad_keys = jnp.einsum(
        "hqk,qhe->khe", grad_scores, queries, preferred_element_type=jnp.float32
    ) * HEAD_DIM ** (-0.5)
    grad_values = jnp.einsum(
        "hqk,qhe->khe", probs.astype(jnp.bfloat16), grad_head, preferred_element_type=jnp.float32
    )
    return (grad_queries, grad_keys, grad_values)


def exact_gelu(value):
    return jax.nn.gelu(value, approximate=False)


def widen_rows(value):
    return lax.all_gather(value, "tensor", axis=1, tiled=True)


def narrow_sums(value):
    return lax.psum_scatter(
        value.astype(jnp.bfloat16), "tensor", scatter_dimension=1, tiled=True
    ).astype(jnp.float32)


def spread_grads(value):
    return lax.all_gather(value, "tensor", axis=1, tiled=True)


def collect_grads(value):
    return lax.psum_scatter(
        value.astype(jnp.bfloat16), "tensor", scatter_dimension=1, tiled=True
    ).astype(jnp.float32)


def close_branch(operand_low, weight_part, formula, summer):
    return summer(jnp.einsum(formula, operand_low, weight_part, preferred_element_type=jnp.float32))


def close_projections(projected_low, qkv_weight):
    return collect_grads(
        jnp.einsum("jnle,jde->nld", projected_low, qkv_weight, preferred_element_type=jnp.float32)
    )


def add_pair(earlier, later):
    return earlier + later


def run_layer(
    rows_in,
    rows_grad,
    lens,
    attn_gain,
    attn_shift,
    qkv_weight,
    qkv_bias,
    out_weight,
    out_bias,
    ffn_gain,
    ffn_shift,
    up_weight,
    up_bias,
    down_weight,
    down_bias,
):
    row_total = rows_in.shape[0]
    head_count = qkv_weight.shape[2] // HEAD_DIM
    rows_float = rows_in.astype(jnp.float32)
    first_norm, normed_one, inv_one = norm_forward(rows_float, attn_gain, attn_shift)
    first_full = widen_rows(first_norm.astype(jnp.bfloat16))
    row_length = first_full.shape[1]
    segment, position = gene_layout(lens, row_length)
    cosine, sine_table = rope_tables(position, HEAD_DIM // 2)
    projected = (
        jnp.einsum("nld,jde->jnle", first_full, qkv_weight, preferred_element_type=jnp.float32)
        + qkv_bias[:, None, None, :]
    )
    shaped = projected.reshape(3, row_total, row_length, head_count, HEAD_DIM)
    queries = rotate_pairs(shaped[0], cosine, sine_table).astype(jnp.bfloat16)
    keys = rotate_pairs(shaped[1], cosine, sine_table).astype(jnp.bfloat16)
    values = shaped[2].astype(jnp.bfloat16)
    heads_out, log_total = lax.map(attend_row, (queries, keys, values, segment))
    head_out = heads_out.reshape(row_total, row_length, head_count * HEAD_DIM).astype(jnp.bfloat16)
    attention = close_branch(head_out, out_weight, "nle,ed->nld", narrow_sums) + out_bias
    middle = rows_float + attention
    second_norm, normed_two, inv_two = norm_forward(middle, ffn_gain, ffn_shift)
    second_full = widen_rows(second_norm.astype(jnp.bfloat16))
    hidden = (
        jnp.einsum("nld,df->nlf", second_full, up_weight, preferred_element_type=jnp.float32)
        + up_bias
    )
    activated, gelu_back = jax.vjp(exact_gelu, hidden)
    act_low = activated.astype(jnp.bfloat16)
    final = middle + close_branch(act_low, down_weight, "nlf,fd->nld", narrow_sums) + down_bias
    grad_final = rows_grad.astype(jnp.float32)
    down_bias_grad = jnp.sum(grad_final, axis=(0, 1))
    final_full = spread_grads(grad_final.astype(jnp.bfloat16))
    down_weight_grad = jnp.einsum(
        "nlf,nld->fd", act_low, final_full, preferred_element_type=jnp.float32
    )
    grad_act = jnp.einsum(
        "nld,fd->nlf", final_full, down_weight, preferred_element_type=jnp.float32
    )
    (grad_hidden,) = gelu_back(grad_act)
    up_bias_grad = jnp.sum(grad_hidden, axis=(0, 1))
    hidden_low = grad_hidden.astype(jnp.bfloat16)
    up_weight_grad = jnp.einsum(
        "nld,nlf->df", second_full, hidden_low, preferred_element_type=jnp.float32
    )
    grad_second = close_branch(hidden_low, up_weight, "nlf,df->nld", collect_grads)
    second_back, ffn_gain_grad, ffn_shift_grad = norm_backward(
        grad_second, normed_two, inv_two, ffn_gain
    )
    grad_middle = grad_final + second_back
    out_bias_grad = jnp.sum(grad_middle, axis=(0, 1))
    middle_full = spread_grads(grad_middle.astype(jnp.bfloat16))
    out_weight_grad = jnp.einsum(
        "nle,nld->ed", head_out, middle_full, preferred_element_type=jnp.float32
    )
    grad_head = jnp.einsum(
        "nld,ed->nle", middle_full, out_weight, preferred_element_type=jnp.float32
    ).astype(jnp.bfloat16)
    grad_head = grad_head.reshape(row_total, row_length, head_count, HEAD_DIM)
    grad_queries, grad_keys, grad_values = lax.map(
        attend_back, (queries, keys, values, segment, log_total, grad_head)
    )
    grad_queries = rotate_pairs(grad_queries, cosine, -sine_table)
    grad_keys = rotate_pairs(grad_keys, cosine, -sine_table)
    grad_projected = jnp.stack([grad_queries, grad_keys, grad_values]).reshape(
        3, row_total, row_length, head_count * HEAD_DIM
    )
    qkv_bias_grad = jnp.sum(grad_projected, axis=(1, 2))
    projected_low = grad_projected.astype(jnp.bfloat16)
    qkv_weight_grad = jnp.einsum(
        "nld,jnle->jde", first_full, projected_low, preferred_element_type=jnp.float32
    )
    grad_first = close_projections(projected_low, qkv_weight)
    first_back, attn_gain_grad, attn_shift_grad = norm_backward(
        grad_first, normed_one, inv_one, attn_gain
    )
    input_grad = (grad_middle + first_back).astype(jnp.bfloat16)
    summed = lax.psum(
        (
            qkv_weight_grad,
            qkv_bias_grad,
            out_weight_grad,
            up_weight_grad,
            up_bias_grad,
            down_weight_grad,
        ),
        "dp",
    )
    (
        qkv_weight_grad,
        qkv_bias_grad,
        out_weight_grad,
        up_weight_grad,
        up_bias_grad,
        down_weight_grad,
    ) = summed
    shared = lax.psum(
        (
            attn_gain_grad,
            attn_shift_grad,
            out_bias_grad,
            ffn_gain_grad,
            ffn_shift_grad,
            down_bias_grad,
        ),
        ("dp", "tensor"),
    )
    (
        attn_gain_grad,
        attn_shift_grad,
        out_bias_grad,
        ffn_gain_grad,
        ffn_shift_grad,
        down_bias_grad,
    ) = shared
    grads_all = (
        attn_gain_grad,
        attn_shift_grad,
        qkv_weight_grad,
        qkv_bias_grad,
        out_weight_grad,
        out_bias_grad,
        ffn_gain_grad,
        ffn_shift_grad,
        up_weight_grad,
        up_bias_grad,
        down_weight_grad,
        down_bias_grad,
    )
    return (final.astype(jnp.bfloat16), input_grad, grads_all)


def body(
    tokens,
    cotangent,
    lengths,
    row_counts,
    attn_gain,
    attn_shift,
    qkv_weight,
    qkv_bias,
    out_weight,
    out_bias,
    ffn_gain,
    ffn_shift,
    up_weight,
    up_bias,
    down_weight,
    down_bias,
    head_weight,
    codon_freq,
):
    slots = tokens.shape[0]
    own_rows = slots - 1
    row_count = row_counts[0]
    live_rows = jnp.arange(slots, dtype=jnp.int32) < row_count
    weights = (
        attn_gain,
        attn_shift,
        qkv_weight,
        qkv_bias,
        out_weight,
        out_bias,
        ffn_gain,
        ffn_shift,
        up_weight,
        up_bias,
        down_weight,
        down_bias,
    )
    device = lax.axis_index("dp")
    offset = prefix(row_counts, "dp", add_pair, jnp.zeros((1,), jnp.int32))[0]
    carried = (offset - device * own_rows).astype(jnp.int32)
    tail_index = row_count - 1
    tail = (
        lax.dynamic_slice_in_dim(tokens, tail_index, 1, 0),
        lax.dynamic_slice_in_dim(cotangent, tail_index, 1, 0),
        lax.dynamic_slice_in_dim(lengths, tail_index, 1, 0),
    )
    arrived = shifted((tail[0], tail[1], tail[2]), "dp", 1)
    first_slot = 1 - carried
    owned_tokens = lax.dynamic_slice_in_dim(
        jnp.concatenate([arrived[0], tokens], axis=0), first_slot, own_rows, 0
    )
    owned_grad = lax.dynamic_slice_in_dim(
        jnp.concatenate([arrived[1], cotangent], axis=0), first_slot, own_rows, 0
    )
    owned_lens = lax.dynamic_slice_in_dim(
        jnp.concatenate([arrived[2], lengths], axis=0), first_slot, own_rows, 0
    )
    owned_out, owned_back, grads_all = run_layer(owned_tokens, owned_grad, owned_lens, *weights)
    returned = shifted((owned_out[0:1], owned_back[0:1]), "dp", -1)
    blank = jnp.zeros(tokens.shape, jnp.bfloat16)
    mixed_rows = lax.dynamic_slice_in_dim(
        jnp.concatenate([owned_out, returned[0], blank], axis=0), carried, slots, 0
    )
    grad_rows = lax.dynamic_slice_in_dim(
        jnp.concatenate([owned_back, returned[1], blank], axis=0), carried, slots, 0
    )
    mixed = jnp.where(live_rows[:, None, None], mixed_rows, jnp.zeros_like(mixed_rows))
    input_grad = jnp.where(live_rows[:, None, None], grad_rows, jnp.zeros_like(grad_rows))
    logits = jnp.einsum("nld,dv->nlv", mixed, head_weight, preferred_element_type=jnp.float32)
    probs = jax.nn.softmax(logits, axis=-1)
    weighted = jnp.sum(probs * live_rows.astype(jnp.float32)[:, None, None], axis=(0, 1))
    mean_prob = weighted / (row_count * tokens.shape[1]).astype(jnp.float32)
    codon_gap = (jnp.log(mean_prob) - jnp.log(codon_freq)).reshape(1, 1, -1)
    return (mixed, input_grad) + tuple(grads_all) + (codon_gap,)


def solution(mesh):
    placed = (
        P("dp", "tensor", None),
        P("dp", "tensor", None),
        P("dp", None),
        P("dp"),
        P(),
        P(),
        P(None, None, "tensor"),
        P(None, "tensor"),
        P("tensor", None),
        P(),
        P(),
        P(),
        P(None, "tensor"),
        P("tensor"),
        P("tensor", None),
        P(),
        P(),
        P(),
    )
    return jax.shard_map(
        body,
        mesh=mesh,
        in_specs=placed,
        out_specs=(
            P("dp", "tensor", None),
            P("dp", "tensor", None),
            P(),
            P(),
            P(None, None, "tensor"),
            P(None, "tensor"),
            P("tensor", None),
            P(),
            P(),
            P(),
            P(None, "tensor"),
            P("tensor"),
            P("tensor", None),
            P(),
            P("dp", "tensor", None),
        ),
        check_vma=False,
    )
```

profile of v0, /device:TPU:0, one launch (start us, length us, event | category | flops | bytes accessed | tf_op | source)
XLA Modules:
  0.0 727.8 jit_solution(14072028957040141071)
XLA Ops:
  9.0 4.9 collective-permute-start
  15.9 11.9 %all-reduce = s32[8]{0:T(128)S(1)} all-reduce(s32[8]{0:T(128)S(1)} %dynamic-update-slice), channel_id=2, replica_groups=mesh['dp'=8,'tensor'=4] {'dp'}, use_global_device_ids=true, to_apply=%add | all-reduce | flops 8 | bytes 64
  27.9 8.8 %while.42 = (s32[]{:T(128)}, s32[1]{0:T(128)}, s32[]{:T(128)}, s32[8,1]{0,1:T(1,128)S(1)}) while((s32[]{:T(128)}, s32[1]{0:T(128)}, s32[]{:T(128)}, s32[8,1]{0,1:T(1,128)S(1)}) %tuple.141), condition=%wide.region_1.2_spmd.clone, body=%wide.region_0.1_spmd.sunk.clone | while | flops 5 | bytes 107 | solution.py:22
  40.8 6.1 collective-permute-start.1
  50.4 19.9 %all-gather.6.cloned.1.call-done = bf16[2,1024,768]{2,1,0:T(8,128)(2,1)} async-done(((bf16[2,256,768]{2,1,0:T(8,128)(2,1)}), bf16[2,1024,768]{2,1,0:T(8,128)(2,1)}) %all-gather.6.cloned.1.call-update) | async-done | bytes 3145744 | tf_op jit(solution)/shard_map/all_gather | solution.py:120
  70.3 4.1 add_bitcast_fusion
  76.6 45.0 %while.43 = (s32[]{:T(128)}, bf16[2,1024,3,64]{1,3,2,0:T(8,128)(2,1)}, f32[2,3,1024,1]{2,1,3,0:T(4,128)}, bf16[2,1024,3,64]{1,3,2,0:T(8,128)(2,1)}, s32[2,1024]{...) while((s32[]{:T(128)}, ...), condition=%wide.region_10.11_spmd.clone, body=%wide.region_7.10_spmd.sunk.clone | while | flops 844100608 | bytes 53676264 | solution.py:186
  77.3 6.0 fusion.188
  83.3 7.4 %fusion.189 = f32[3,1024]{1,0:T(4,128)S(1)} fusion(f32[3,1024,1024]{1,2,0:T(8,128)} %get-tuple-element.452, f32[3,1024]{1,0:T(4,128)S(1)} %get-tuple-element.453, pred[1024,1024]{0,1:T(8,128)(4,1)S(1)} %broadcast_compare_fusion.6), kind=kLoop, calls=%fused_computation.5.clone.1.clone | loop fusion | flops 12579840 | bytes 13656064 | tf_op jit(solution)/shard_map/while/body/eval_jaxpr/reduce_sum | solution.py:89
  90.8 6.8 fusion.190
  99.8 6.0 fusion.188
  105.8 7.4 %fusion.189 = f32[3,1024]{1,0:T(4,128)S(1)} fusion(f32[3,1024,1024]{1,2,0:T(8,128)} %get-tuple-element.452, f32[3,1024]{1,0:T(4,128)S(1)} %get-tuple-element.453, pred[1024,1024]{0,1:T(8,128)(4,1)S(1)} %broadcast_compare_fusion.6), kind=kLoop, calls=%fused_computation.5.clone.1.clone | loop fusion | flops 12579840 | bytes 13656064 | tf_op jit(solution)/shard_map/while/body/eval_jaxpr/reduce_sum | solution.py:89
  113.3 6.8 fusion.190
  121.6 4.2 convolution_convert_fusion
  125.9 38.1 %reduce-scatter.5.cloned.1.call-done = bf16[2,256,768]{2,1,0:T(8,128)(2,1)} async-done(((bf16[2,1024,768]{2,1,0:T(8,128)(2,1)}), bf16[2,256,768]{2,1,0:T(8,128)(2,1)}) %reduce-scatter.5.cloned.1.call-update) | async-done | bytes 786448 | tf_op jit(solution)/shard_map/reduce_scatter | solution.py:124
  170.8 3.4 collective-permute-start.3
  174.2 8.4 %collective-permute-done.3 = bf16[1,256,768]{2,1,0:T(8,128)(2,1)S(1)} collective-permute-done((bf16[1,256,768]{2,1,0:T(8,128)(2,1)S(1)}, bf16[1,256,768]{2,1,0:T(8,128)(2,1)S(1)}, u32[]{:S(2)}, u32[]{:S(2)}) %collective-permute-start.3) | collective-permute-done | bytes 393248 | tf_op jit(solution)/shard_map/ppermute | solution.py:28
  185.9 12.5 %all-gather.8.cloned.1.call-done = bf16[2,1024,768]{2,1,0:T(8,128)(2,1)} async-done(((bf16[2,256,768]{2,1,0:T(8,128)(2,1)}), bf16[2,1024,768]{2,1,0:T(8,128)(2,1)}) %all-gather.8.cloned.1.call-update) | async-done | bytes 3145744 | tf_op jit(solution)/shard_map/all_gather | solution.py:120
  198.4 6.4 fusion.95
  204.8 2.7 copy-done.19
  207.5 15.7 %multiply_convert_fusion.1 = (bf16[2,1024,768]{2,1,0:T(8,128)(2,1)}, f32[2,1024,768]{2,1,0:T(8,128)}) fusion(f32[2,1024,768]{2,1,0:T(8,128)S(1)} %get-tuple-element.290, f32[768]{0:T(1024)S(1)} %copy-done.72, u8[1024,768]{1,0:T(8,128)(4,1)S(1)} %get-tuple-element.193, u8[1024,768]{1,0:T(8,128)(4,1)S(1)} %get-tuple-element.192), kind=kLoop, calls=%fused_computation.74 | loop fusion | flops 111673344 | bytes 17304576 | tf_op jit(solution)/shard_map/convert_element_type | solution.py:197
  223.2 5.8 all-gather.10.cloned.1.call-done
  229.1 11.0 %fusion.133 = (f32[768]{0:T(1024)}, bf16[2,1024,768]{2,1,0:T(8,128)(2,1)S(1)}) fusion(f32[2,1024,768]{2,1,0:T(8,128)} %get-tuple-element.262, bf16[2,1024,768]{2,1,0:T(8,128)(2,1)} %all-gather.10.cloned.1.call-done, bf16[768,768]{1,0:T(8,128)(2,1)} %param.38, f32[2,1024,768]{2,1,0:T(8,128)} %copy-done.19, f32[768]{0:T(1024)} %param.37), kind=kOutput, calls=%fused_computation.220 | convolution fusion | flops 2441084160 | bytes 20060160 | tf_op jit(solution)/shard_map/nld,fd->nlf/dot_general | solution.py:205
  241.7 4.0 convolution_convert_fusion.1
  246.0 37.9 %reduce-scatter.9.cloned.1.call-done = bf16[2,256,768]{2,1,0:T(8,128)(2,1)} async-done(((bf16[2,1024,768]{2,1,0:T(8,128)(2,1)}), bf16[2,256,768]{2,1,0:T(8,128)(2,1)}) %reduce-scatter.9.cloned.1.call-update) | async-done | bytes 786448 | tf_op jit(solution)/shard_map/reduce_scatter | solution.py:134
  288.9 28.6 %all-gather.12.cloned.1.call-done = bf16[2,1024,768]{2,1,0:T(8,128)(2,1)} async-done(((bf16[2,256,768]{2,1,0:T(8,128)(2,1)}), bf16[2,1024,768]{2,1,0:T(8,128)(2,1)}) %all-gather.12.cloned.1.call-update) | async-done | bytes 3145744 | tf_op jit(solution)/shard_map/all_gather | solution.py:130
  317.5 3.1 convolution_convert_fusion.3
  320.6 49.9 %while.44 = (s32[]{:T(128)}, f32[2,1024,3,64]{1,3,2,0:T(8,128)}, f32[2,1024,3,64]{1,3,2,0:T(8,128)}, f32[2,1024,3,64]{1,3,2,0:T(8,128)}, bf16[2,1024,3,64]{1,3,2...) while((s32[]{:T(128)}, f32[2,1024,3,64]{1,3,2,0:T(8,128)}, ...), condition=%wide.region_20.21_spmd.clone, body=%wide.region_18.20_spmd.sunk.clone | while | flops 2061890560 | bytes 141538624 | solution.py:228
  323.2 3.6 fusion.202
  326.8 7.2 multiply_reduce_fusion.4
  334.0 7.1 multiply_convert_fusion.4
  348.1 3.6 fusion.202
  351.8 7.2 multiply_reduce_fusion.4
  359.0 7.1 multiply_convert_fusion.4
  375.9 4.3 bitcast_convert_fusion
  381.4 6.2 convolution_convert_fusion.2
  387.7 7.7 %convolution_bitcast_fusion = f32[768,768]{1,0:T(8,128)} fusion(bf16[2,1024,768]{2,1,0:T(8,128)(2,1)} %get-tuple-element.261, bf16[2,1024,768]{2,1,0:T(8,128)(2,1)} %all-gather.10.cloned.1.call-done), kind=kOutput, calls=%fused_computation.124 | convolution fusion | flops 2415919104 | bytes 8650752 | tf_op jit(solution)/shard_map/nlf,nld->fd/dot_general | solution.py:202
  395.4 4.2 convolution_bitcast_fusion.1
  401.7 3.2 fusion.96
  405.1 13.2 %reduce-scatter.11.cloned.1.call-done = bf16[2,256,768]{2,1,0:T(8,128)(2,1)} async-done(((bf16[2,1024,768]{2,1,0:T(8,128)(2,1)}), bf16[2,256,768]{2,1,0:T(8,128)(2,1)}) %reduce-scatter.11.cloned.1.call-update) | async-done | bytes 786448 | tf_op jit(solution)/shard_map/reduce_scatter | solution.py:134
  418.4 4.2 fusion.90
  422.6 36.4 %reduce-scatter.7.cloned.1.call-done = bf16[2,256,768]{2,1,0:T(8,128)(2,1)} async-done(((bf16[2,1024,768]{2,1,0:T(8,128)(2,1)}), bf16[2,256,768]{2,1,0:T(8,128)(2,1)}) %reduce-scatter.7.cloned.1.call-update) | async-done | bytes 786448 | tf_op jit(solution)/shard_map/reduce_scatter | solution.py:124
  459.0 3.1 fusion.84
  467.6 59.1 %all-reduce.2 = (f32[3,192]{1,0:T(4,128)}, f32[768]{0:T(1024)}) all-reduce(f32[3,192]{1,0:T(4,128)S(1)} %fusion.61, f32[768]{0:T(1024)S(1)} %copy-done.73), channel_id=1, replica_groups=mesh['dp'=8,'tensor'=4] {'dp'}, use_global_device_ids=true, to_apply=%region_30.31 | all-reduce | flops 1344 | bytes 10752 | tf_op jit(solution)/shard_map/psum | solution.py:246
  526.7 42.4 %all-reduce.1 = (f32[768]{0:T(1024)}, f32[768]{0:T(1024)}, f32[768]{0:T(1024)}, f32[768]{0:T(1024)}, f32[768]{0:T(1024)}, /*index=5*/f32[768]{0:T(1024)}) all-reduce(f32[768]{0:T(1024)S(1)} %copy-done.68, f32[768]{0:T(1024)S(1)} %copy-done.69, f32[768]{0:T(1024)S(1)} %get-tuple-element.195, ...), channel_id=1, replica_groups=mesh['dp'=8,'tensor'=4] {'dp','tensor'}, use_global_device_ids=true, to_apply=%region_25.26 | all-reduce | flops 4608 | bytes 36864 | tf_op jit(solution)/shard_map/psum | solution.py:265
  569.2 2.7 fusion.104
  574.1 139.1 %all-reduce.6.cloned.1.call-done = (f32[3,768,192]{1,2,0:T(8,128)}, f32[192,768]{1,0:T(8,128)}, f32[768,768]{1,0:T(8,128)}, f32[768,768]{1,0:T(8,128)}) async-done(((f32[3,768,192]{1,2,0:T(8,128)}, f32[192,768]{1,0:T(8,128)}, f32[768,768]{1,0:T(8,128)}, f32[768,768]{1,0:T(8,128)}), (f32[3,768,192]{1,2,0:T(8,128)}, f32[192,768]{1,0:T(8,128)}, f32[768,768]{1,0:T(8,128)}, ...) | async-done | bytes 7077904 | tf_op jit(solution)/shard_map/psum | solution.py:246
  713.1 2.9 copy.96
  (294 shorter events, 73.2 us)
Async XLA Ops:
  7.2 191.2 %copy-start = (bf16[768,768]{1,0:T(8,128)(2,1)S(1)}, bf16[768,768]{1,0:T(8,128)(2,1)}, u32[]{:S(2)}) copy-start(bf16[768,768]{1,0:T(8,128)(2,1)} %param.36) | copy-start | bytes 3538948
  7.2 32.3 %copy-start.60 = (f32[768]{0:T(1024)S(1)}, f32[768]{0:T(1024)}, u32[]{:S(2)}) copy-start(f32[768]{0:T(1024)} %param.28) | copy-start | bytes 9220
  7.2 32.3 %copy-start.71 = (f32[768]{0:T(1024)S(1)}, f32[768]{0:T(1024)}, u32[]{:S(2)}) copy-start(f32[768]{0:T(1024)} %param.29) | copy-start | bytes 9220
  7.2 63.1 %all-gather.6.cloned.1.call-start = ((), (), s32[]{:S(2)}) async-start(), calls=%async_computation.4 | async-start | bytes 3932160 | tf_op jit(solution)/shard_map/all_gather | solution.py:120
  9.0 27.7 %collective-permute-start = (bf16[1,256,768]{2,1,0:T(8,128)(2,1)S(1)}, bf16[1,256,768]{2,1,0:T(8,128)(2,1)S(1)}, u32[]{:S(2)}, u32[]{:S(2)}) collective-permute-start(bf16[1,256,768]{2,1,0:T(8,128)(2,1)S(1)} %constant_dynamic-slice_fusion.6), channel_id=1, source_target_pairs={{0,4},{4,8},{8,12},{12,16},{16,20},{20,24},{24,28},{1,5},{5,9},{9,... | collective-permute-start | bytes 1179656 | tf_op jit(solution)/shard_map/ppermute | solution.py:28
  38.2 247.7 %copy-start.2 = (bf16[2,256,768]{2,1,0:T(8,128)(2,1)}, bf16[2,256,768]{2,1,0:T(8,128)(2,1)S(1)}, u32[]{:S(2)}) copy-start(bf16[2,256,768]{2,1,0:T(8,128)(2,1)S(1)} %get-tuple-element.264) | copy-start | bytes 2359300
  38.2 32.1 %copy-start.80 = (f32[3,192]{1,0:T(4,128)S(1)}, f32[3,192]{1,0:T(4,128)}, u32[]{:S(2)}) copy-start(f32[3,192]{1,0:T(4,128)} %param.31) | copy-start | bytes 6916
  40.8 123.2 %reduce-scatter.5.cloned.1.call-start = ((), (), s32[]{:S(2)}) async-start(), calls=%async_computation.5 | async-start | bytes 3932160 | tf_op jit(solution)/shard_map/reduce_scatter | solution.py:124
  40.8 7.4 %collective-permute-start.1 = (s32[1,4]{1,0:T(1,128)S(1)}, s32[1,4]{1,0:T(1,128)S(1)}, u32[]{:S(2)}, u32[]{:S(2)}) collective-permute-start(s32[1,4]{1,0:T(1,128)S(1)} %constant_dynamic-slice_fusion.5), channel_id=1, source_target_pairs={{0,4},{4,8},{8,12},{12,16},{16,20},{20,24},{24,28},{1,5},{5,9},{9,... | collective-permute-start | bytes 56 | tf_op jit(solution)/shard_map/ppermute | solution.py:28
  50.4 25.5 %copy-start.32 = (f32[2,1024,32]{1,2,0:T(8,128)}, f32[2,1024,32]{1,2,0:T(8,128)S(1)}, u32[]{:S(2)}) copy-start(f32[2,1024,32]{1,2,0:T(8,128)S(1)} %get-tuple-element.289) | copy-start | bytes 786436
  125.8 38.1 %copy-start.48 = (f32[768]{0:T(1024)S(1)}, f32[768]{0:T(1024)}, u32[]{:S(2)}) copy-start(f32[768]{0:T(1024)} %param.33) | copy-start | bytes 9220
  125.8 41.9 %copy-start.50 = (f32[768]{0:T(1024)S(1)}, f32[768]{0:T(1024)}, u32[]{:S(2)}) copy-start(f32[768]{0:T(1024)} %param.34) | copy-start | bytes 9220
  125.8 72.6 %all-gather.8.cloned.1.call-start = ((), (), s32[]{:S(2)}) async-start(), calls=%async_computation.6 | async-start | bytes 3932160 | tf_op jit(solution)/shard_map/all_gather | solution.py:120
  169.7 59.3 %all-gather.10.cloned.1.call-start = ((), (), s32[]{:S(2)}) async-start(), calls=%async_computation.8 | async-start | bytes 3932160 | tf_op jit(solution)/shard_map/all_gather | solution.py:130
  170.8 11.8 %collective-permute-start.3 = (bf16[1,256,768]{2,1,0:T(8,128)(2,1)S(1)}, bf16[1,256,768]{2,1,0:T(8,128)(2,1)S(1)}, u32[]{:S(2)}, u32[]{:S(2)}) collective-permute-start(bf16[1,256,768]{2,1,0:T(8,128)(2,1)S(1)} %constant_dynamic-slice_fusion.3), channel_id=1, source_target_pairs={{0,4},{4,8},{8,12},{12,16},{16,20},{20,24},{24,28},{1,5},{5,9},{9,... | collective-permute-start | bytes 1179656 | tf_op jit(solution)/shard_map/ppermute | solution.py:28
  185.5 98.3 %reduce-scatter.9.cloned.1.call-start = ((), (), s32[]{:S(2)}) async-start(), calls=%async_computation.9 | async-start | bytes 3932160 | tf_op jit(solution)/shard_map/reduce_scatter | solution.py:134
  198.4 9.1 %copy-start.72 = (f32[768]{0:T(1024)S(1)}, f32[768]{0:T(1024)}, u32[]{:S(2)}) copy-start(f32[768]{0:T(1024)} %param.37) | copy-start | bytes 9220
  245.7 41.3 %copy-start.8 = (bf16[3,256,768]{2,1,0:T(8,128)(2,1)S(1)}, bf16[3,256,768]{2,1,0:T(8,128)(2,1)}, u32[]{:S(2)}) copy-start(bf16[3,256,768]{2,1,0:T(8,128)(2,1)} %param.25) | copy-start | bytes 3538948
  245.7 71.8 %all-gather.12.cloned.1.call-start = ((), (), s32[]{:S(2)}) async-start(), calls=%async_computation.10 | async-start | bytes 3932160 | tf_op jit(solution)/shard_map/all_gather | solution.py:130
  288.8 31.8 %copy-start.7 = (bf16[2,1024,3,64]{1,3,2,0:T(8,128)(2,1)S(1)}, bf16[2,1024,3,64]{1,3,2,0:T(8,128)(2,1)}, u32[]{:S(2)}) copy-start(bf16[2,1024,3,64]{1,3,2,0:T(8,128)(2,1)} %copy-done.6) | copy-start | bytes 2359300
  288.8 31.8 %copy-start.15 = (bf16[2,1024,3,64]{1,3,2,0:T(8,128)(2,1)S(1)}, bf16[2,1024,3,64]{1,3,2,0:T(8,128)(2,1)}, u32[]{:S(2)}) copy-start(bf16[2,1024,3,64]{1,3,2,0:T(8,128)(2,1)} %get-tuple-element.586) | copy-start | bytes 2359300
  288.9 31.8 %copy-start.47 = (f32[2,3,1024,1]{2,1,3,0:T(4,128)S(1)}, f32[2,3,1024,1]{2,1,3,0:T(4,128)}, u32[]{:S(2)}) copy-start(f32[2,3,1024,1]{2,1,3,0:T(4,128)} %get-tuple-element.526) | copy-start | bytes 73732
  288.9 129.4 %reduce-scatter.11.cloned.1.call-start = ((), (), s32[]{:S(2)}) async-start(), calls=%async_computation.11 | async-start | bytes 3932160 | tf_op jit(solution)/shard_map/reduce_scatter | solution.py:134
  320.6 49.9 %copy-start.33 = (f32[2,1024,32]{1,2,0:T(8,128)S(1)}, f32[2,1024,32]{1,2,0:T(8,128)}, u32[]{:S(2)}) copy-start(f32[2,1024,32]{1,2,0:T(8,128)} %copy-done.32) | copy-start | bytes 786436
  373.1 28.2 %copy-start.20 = (f32[2,1024,3,64]{1,3,2,0:T(8,128)}, f32[2,1024,3,64]{1,3,2,0:T(8,128)S(1)}, u32[]{:S(2)}) copy-start(f32[2,1024,3,64]{1,3,2,0:T(8,128)S(1)} %pad_maximum_fusion.1) | copy-start | bytes 4718596
  380.2 78.8 %reduce-scatter.7.cloned.1.call-start = ((), (), s32[]{:S(2)}) async-start(), calls=%async_computation.7 | async-start | bytes 3932160 | tf_op jit(solution)/shard_map/reduce_scatter | solution.py:124
  387.7 325.4 %all-reduce.6.cloned.1.call-start = ((), (), s32[]{:S(2)}) async-start(), calls=%async_computation.12 | async-start | bytes 14155776 | tf_op jit(solution)/shard_map/psum | solution.py:246
  404.9 13.4 %copy-start.3 = (bf16[2,256,768]{2,1,0:T(8,128)(2,1)S(1)}, bf16[2,256,768]{2,1,0:T(8,128)(2,1)}, u32[]{:S(2)}) copy-start(bf16[2,256,768]{2,1,0:T(8,128)(2,1)} %copy-done.2) | copy-start | bytes 2359300
  404.9 13.4 %copy-start.5 = (bf16[2,256,768]{2,1,0:T(8,128)(2,1)S(1)}, bf16[2,256,768]{2,1,0:T(8,128)(2,1)}, u32[]{:S(2)}) copy-start(bf16[2,256,768]{2,1,0:T(8,128)(2,1)} %reduce-scatter.5.cloned.1.call-done) | copy-start | bytes 2359300
  404.9 13.4 %copy-start.9 = (bf16[3,256,768]{2,1,0:T(8,128)(2,1)S(1)}, bf16[3,256,768]{2,1,0:T(8,128)(2,1)}, u32[]{:S(2)}) copy-start(bf16[3,256,768]{2,1,0:T(8,128)(2,1)} %param.25) | copy-start | bytes 3538948
  404.9 13.4 %copy-start.18 = (bf16[1,256,768]{2,1,0:T(8,128)(2,1)S(1)}, bf16[1,256,768]{2,1,0:T(8,128)(2,1)}, u32[]{:S(2)}) copy-start(bf16[1,256,768]{2,1,0:T(8,128)(2,1)} %copy-done.16) | copy-start | bytes 1179652
  404.9 13.4 %copy-start.49 = (f32[768]{0:T(1024)S(1)}, f32[768]{0:T(1024)}, u32[]{:S(2)}) copy-start(f32[768]{0:T(1024)} %param.33) | copy-start | bytes 9220
  404.9 13.4 %copy-start.51 = (f32[768]{0:T(1024)S(1)}, f32[768]{0:T(1024)}, u32[]{:S(2)}) copy-start(f32[768]{0:T(1024)} %param.34) | copy-start | bytes 9220
  404.9 13.4 %copy-start.54 = (f32[2,256]{1,0:T(2,128)S(1)}, f32[2,256]{1,0:T(2,128)}, u32[]{:S(2)}) copy-start(f32[2,256]{1,0:T(2,128)} %copy-done.52) | copy-start | bytes 6148
  405.0 13.4 %copy-start.57 = (f32[2,256]{1,0:T(2,128)S(1)}, f32[2,256]{1,0:T(2,128)}, u32[]{:S(2)}) copy-start(f32[2,256]{1,0:T(2,128)} %copy-done.55) | copy-start | bytes 6148
  405.0 13.4 %copy-start.59 = (f32[2,256]{1,0:T(2,128)S(1)}, f32[2,256]{1,0:T(2,128)}, u32[]{:S(2)}) copy-start(f32[2,256]{1,0:T(2,128)} %copy-done.58) | copy-start | bytes 6148
  405.0 13.4 %copy-start.61 = (f32[768]{0:T(1024)S(1)}, f32[768]{0:T(1024)}, u32[]{:S(2)}) copy-start(f32[768]{0:T(1024)} %param.28) | copy-start | bytes 9220
  405.0 13.4 %copy-start.63 = (f32[2,256]{1,0:T(2,128)S(1)}, f32[2,256]{1,0:T(2,128)}, u32[]{:S(2)}) copy-start(f32[2,256]{1,0:T(2,128)} %copy-done.62) | copy-start | bytes 6148
  405.0 13.4 %copy-start.65 = (f32[2,256]{1,0:T(2,128)S(1)}, f32[2,256]{1,0:T(2,128)}, u32[]{:S(2)}) copy-start(f32[2,256]{1,0:T(2,128)} %copy-done.64) | copy-start | bytes 6148
  405.0 13.4 %copy-start.67 = (f32[2,256]{1,0:T(2,128)S(1)}, f32[2,256]{1,0:T(2,128)}, u32[]{:S(2)}) copy-start(f32[2,256]{1,0:T(2,128)} %copy-done.66) | copy-start | bytes 6148
  405.1 53.9 %copy-start.70 = (f32[768]{0:T(1024)S(1)}, f32[768]{0:T(1024)}, u32[]{:S(2)}) copy-start(f32[768]{0:T(1024)} %param.39) | copy-start | bytes 9220
  463.1 105.9 %collective-permute-start.2 = (bf16[1,256,768]{2,1,0:T(8,128)(2,1)S(1)}, bf16[1,256,768]{2,1,0:T(8,128)(2,1)S(1)}, u32[]{:S(2)}, u32[]{:S(2)}) collective-permute-start(bf16[1,256,768]{2,1,0:T(8,128)(2,1)S(1)} %slice.63), channel_id=1, source_target_pairs={{4,0},{8,4},{12,8},{16,12},{20,16},{24,20},{28,24},{5,1},{9,5},{13... | collective-permute-start | bytes 1179656 | tf_op jit(solution)/shard_map/ppermute | solution.py:28
  464.5 104.5 %collective-permute-start.4 = (bf16[1,256,768]{2,1,0:T(8,128)(2,1)S(1)}, bf16[1,256,768]{2,1,0:T(8,128)(2,1)S(1)}, u32[]{:S(2)}, u32[]{:S(2)}) collective-permute-start(bf16[1,256,768]{2,1,0:T(8,128)(2,1)S(1)} %slice.64), channel_id=1, source_target_pairs={{4,0},{8,4},{12,8},{16,12},{20,16},{24,20},{28,24},{5,1},{9,5},{13... | collective-permute-start | bytes 1179656 | tf_op jit(solution)/shard_map/ppermute | solution.py:28
  466.9 59.7 %copy-start.68 = (f32[768]{0:T(1024)S(1)}, f32[768]{0:T(1024)}, u32[]{:S(2)}) copy-start(f32[768]{0:T(1024)} %get-tuple-element.205) | copy-start | bytes 9220
  467.0 59.7 %copy-start.69 = (f32[768]{0:T(1024)S(1)}, f32[768]{0:T(1024)}, u32[]{:S(2)}) copy-start(f32[768]{0:T(1024)} %get-tuple-element.206) | copy-start | bytes 9220
  467.0 102.2 %copy-start.26 = (bf16[2,256,768]{2,1,0:T(8,128)(2,1)S(1)}, bf16[2,256,768]{2,1,0:T(8,128)(2,1)}, u32[]{:S(2)}) copy-start(bf16[2,256,768]{2,1,0:T(8,128)(2,1)} %copy-done.25) | copy-start | bytes 2359300
  467.0 102.2 %copy-start.28 = (bf16[2,256,768]{2,1,0:T(8,128)(2,1)S(1)}, bf16[2,256,768]{2,1,0:T(8,128)(2,1)}, u32[]{:S(2)}) copy-start(bf16[2,256,768]{2,1,0:T(8,128)(2,1)} %copy-done.27) | copy-start | bytes 2359300
  571.9 144.2 %copy-start.43 = (bf16[3,256,768]{2,1,0:T(8,128)(2,1)}, bf16[3,256,768]{2,1,0:T(8,128)(2,1)S(1)}, u32[]{:S(2)}) copy-start(bf16[3,256,768]{2,1,0:T(8,128)(2,1)S(1)} %get-tuple-element.549) | copy-start | bytes 3538948
  (61 other events, 209.5 us)
Sparse Core Ops, SparseCore 0:
  40.9 29.4 all-gather.5
  125.9 37.9 reduce-scatter.4
  169.9 28.5 all-gather.7
  200.5 28.5 all-gather.9
  245.9 37.9 reduce-scatter.8
  288.9 28.5 all-gather.11
  380.3 37.9 reduce-scatter.10
  421.0 37.9 reduce-scatter.6
  464.6 248.4 all-reduce.5
where the time goes:
time: 739 us; the launch traced here: 728 us
  waiting for transfers between devices  340 us (46%)
  matrix products  119 us (16%)
  blocking collectives  113 us (15%)
  other arithmetic  79.9 us (11%)
  local copies, waits for them, and re-layouts  36 us (5%)
  starting transfers between devices  18 us (2%)
  between operations  15.9 us (2%)
    psum x1, waiting for transfers between devices, run_layer(): lax.psum((qkv_weight_grad, qkv_bias_grad, out_weight_grad, up_weight_grad...  139 us
    reduce_scatter x2, waiting for transfers between devices, narrow_sums(): lax.psum_scatter(value.astype(jnp.bfloat16), 'tensor', scatter_dimension=...  74.5 us
    psum x1, blocking collectives, run_layer(): lax.psum((qkv_weight_grad, qkv_bias_grad, out_weight_grad, up_weight_grad...  59.1 us
    reduce_scatter x2, waiting for transfers between devices, collect_grads(): lax.psum_scatter(value.astype(jnp.bfloat16), 'tensor', scatter_dimension=...  51.1 us
    psum x1, blocking collectives, run_layer(): lax.psum((attn_gain_grad, attn_shift_grad, out_bias_grad, ffn_gain_grad,...  42.4 us
    all_gather x2, waiting for transfers between devices, spread_grads(): return lax.all_gather(value, 'tensor', axis=1, tiled=True)  34.4 us
    all_gather x2, waiting for transfers between devices, widen_rows(): return lax.all_gather(value, 'tensor', axis=1, tiled=True)  32.4 us
    unnamed x153, local copies, waits for them, and re-layouts  23 us
  transfers between devices with their start and end apart: 14, of which 11 were waited for; matrix products, arithmetic and copies ran while one was open for 10% of the time, Pallas kernels for 0%

commit v1 on v0

v1 whole, which is shorter than its diff:
```python
import functools

import jax
import jax.numpy as jnp
import numpy as np
from jax import lax
from jax.experimental import pallas as pl
from jax.experimental.pallas import tpu as pltpu
from jax.sharding import PartitionSpec as P

HEAD_DIM = 64
EPS = 1e-05
BASE = 10000.0
F32 = jnp.float32
BF16 = jnp.bfloat16
MESH = pl.DeviceIdType.MESH
LANE = 128
CHUNK = 64
FAR = -1e30
MASK_AT = 64
TOTAL_AT = 68


def dot_nn(a, b):
    return lax.dot_general(a, b, (((1,), (0,)), ((), ())), preferred_element_type=F32)


def dot_nt(a, b):
    return lax.dot_general(a, b, (((1,), (1,)), ((), ())), preferred_element_type=F32)


def dot_tn(a, b):
    return lax.dot_general(a, b, (((0,), (0,)), ((), ())), preferred_element_type=F32)


def lanes(shape):
    return lax.broadcasted_iota(jnp.int32, shape, 1)


def three_parts(value):
    high = value.astype(BF16).astype(F32)
    rest = value - high
    middle = rest.astype(BF16).astype(F32)
    return high, middle, rest - middle


def normalize(value):
    average = jnp.mean(value, -1, keepdims=True)
    centred = value - average
    inv_std = lax.rsqrt(jnp.mean(centred * centred, -1, keepdims=True) + EPS)
    return centred * inv_std, inv_std


def norm_back(incoming, normed, inv_std, gain):
    scaled = incoming * gain
    return inv_std * (
        scaled
        - jnp.mean(scaled, -1, keepdims=True)
        - normed * jnp.mean(scaled * normed, -1, keepdims=True)
    )


def swap_halves(value):
    lane = lanes(value.shape)
    return jnp.where(lane < 32, pltpu.roll(value, 96, 1), pltpu.roll(value, 32, 1))


class Copies:
    def __init__(self, send, recv):
        self.send, self.recv, self.count = send, recv, 0

    def make(self, src, dst, device):
        at = self.count
        self.count += 1
        return functools.partial(
            pltpu.make_async_remote_copy,
            src_ref=src,
            dst_ref=dst,
            send_sem=self.send.at[at],
            recv_sem=self.recv.at[at],
            device_id=device,
            device_id_type=MESH,
        )


class Reduce:
    def __init__(self, copies, ref, land, out, store_sem, rows, order, d, t):
        self.ref, self.land = ref, land
        self.plan = []
        offset, used = 0, 0
        backs = []
        for bit in order:
            partner = (d ^ (1 << bit), t)
            side = (d >> bit) & 1
            if rows % 32 == 0:
                half = rows // 2
                keep = offset + half * side
                give = offset + half * (1 - side)
                copy = copies.make(self.at(ref, give, half), land.at[pl.ds(used, half)], partner)
                self.plan.append((copy, keep, half, used))
                backs.append((partner, keep, half))
                used, offset, rows = used + half, keep, half
            else:
                copy = copies.make(self.at(ref, offset, rows), land.at[pl.ds(used, rows)], partner)
                self.plan.append((copy, offset, rows, used))
                used += rows
        self.adds = len(self.plan)
        source, target = self.at(ref, offset, rows), self.at(out, offset, rows)
        self.store = functools.partial(pltpu.make_async_copy, source, target, store_sem)
        for i, (partner, keep, half) in enumerate(reversed(backs)):
            own = self.at(ref if i == 0 else out, keep, half)
            self.plan.append((copies.make(own, self.at(out, keep, half), partner), keep, half, 0))
        self.place = 0

    @staticmethod
    def land_rows(rows, steps):
        used = 0
        for _ in range(steps):
            if rows % 32 == 0:
                rows //= 2
            used += rows
        return used

    @staticmethod
    def at(ref, offset, rows):
        if not isinstance(offset, int):
            offset = pl.multiple_of(offset, 16)
        return ref.at[pl.ds(offset, rows)]

    def start(self):
        self.plan[0][0]().start()

    def left(self):
        return len(self.plan) - self.place

    def tick(self):
        if self.place >= len(self.plan):
            return
        copy, keep, rows, used = self.plan[self.place]
        copy().wait()
        if self.place < self.adds:
            step = max(s for s in (16, 32, 48, 64, 96) if rows % s == 0)

            def add(i, _):
                here = pl.ds(pl.multiple_of(keep + i * step, 16), step)
                there = pl.ds(pl.multiple_of(used + i * step, 16), step)
                total = self.ref[here].astype(F32) + self.land[there].astype(F32)
                self.ref[here] = total.astype(BF16)
                return _

            lax.fori_loop(0, rows // step, add, None)
        if self.place == self.adds - 1:
            self.store().start()
        if self.place == self.adds or (self.place + 1 == len(self.plan) and self.place < self.adds):
            self.store().wait()
        self.place += 1
        if self.place < len(self.plan):
            self.plan[self.place][0]().start()


def layer_kernel(
    n_dp,
    slots,
    quarter,
    features,
    count_ref,
    lens_ref,
    tok_ref,
    cotan_ref,
    wqkv_ref,
    bqkv_ref,
    wout_ref,
    wup_ref,
    wdown_ref,
    bup_ref,
    vec_ref,
    head_ref,
    freq_ref,
    rope_ref,
    base_ref,
    line_ref,
    mixed_out,
    grad_out,
    gdown_out,
    gup_out,
    gout_out,
    gqkv_out,
    small_out,
    codon_out,
    n1,
    n2,
    cot,
    gm,
    heads_q,
    heads_k,
    heads_v,
    head_out,
    head_grad,
    dq_acc,
    dp_low,
    act,
    slope,
    part,
    land_core,
    land_x,
    mid,
    gmid,
    table_c,
    table_s,
    wc,
    bc,
    woe,
    tok_b,
    got_cot,
    scan_mine,
    scan_land,
    lens_mine,
    lens_land,
    gdown,
    gup,
    gout,
    gqkv,
    land_down,
    land_up,
    back_mixed,
    back_grad,
    sums,
    sums_land,
    bias_acc,
    send_sems,
    recv_sems,
    out_sems,
):
    d, t = lax.axis_index("dp"), lax.axis_index("tensor")
    core, across = (d, t ^ 1), (d, t ^ 2)
    own_rows = slots - 1
    dp_steps = n_dp.bit_length() - 1
    copies = Copies(send_sems, recv_sems)

    attn_gain, attn_shift = vec_ref[0:1], vec_ref[1:2]
    out_bias, ffn_gain, ffn_shift, down_bias = (vec_ref[i : i + 1] for i in range(2, 6))

    barrier = pltpu.get_barrier_semaphore()
    greeted = [core, across]
    for k in range(dp_steps):
        greeted.append((d ^ (1 << k), t))
        greeted.append(((d + (1 << k)) % n_dp, t))
        greeted.append(((d + n_dp - (1 << k)) % n_dp, t))
    for other in greeted:
        pl.semaphore_signal(barrier, inc=1, device_id=other, device_id_type=MESH)
    pl.semaphore_wait(barrier, len(greeted))

    def over_chunks(rows, body, step=CHUNK):
        def run(i, _):
            body(pl.ds(pl.multiple_of(i * step, step), step))
            return _

        lax.fori_loop(0, rows // step, run, None)

    mixed, ingrad = n2.at[0, pl.ds(0, slots)], n2.at[1, pl.ds(0, slots)]
    land_qkv = act.at[0, :, pl.ds(0, 5 * LANE)]
    land_out = act.at[1]

    tail_tok, tail_cot = mixed.at[slots - 1], ingrad.at[slots - 1]
    count = count_ref[0]
    count_wide = jnp.full((CHUNK, features), count, jnp.int32)

    def pick_tail(rows):
        for source, target in ((tok_ref, tail_tok), (cotan_ref, tail_cot)):
            value = source[slots - 1, rows].astype(F32)
            for slot in range(slots - 2, -1, -1):
                value = jnp.where(count_wide == slot + 1, source[slot, rows].astype(F32), value)
            target[rows] = value.astype(BF16)

    over_chunks(quarter, pick_tail)
    after, before = (d + 1, t), (d - 1, t)
    send_tok = copies.make(tail_tok, tok_b, after)
    send_cot = copies.make(tail_cot, got_cot, after)
    send_lens = copies.make(lens_mine, lens_land, after)

    def lens_tile(slot):
        row_at = lax.broadcasted_iota(jnp.int32, (8, LANE), 0)
        tile = jnp.zeros((8, LANE), jnp.int32)
        for gene in range(4):
            tile = jnp.where(row_at == gene, lens_ref[slot, gene], tile)
        return tile

    tail_lens = lens_tile(slots - 1)
    for slot in range(slots - 2, -1, -1):
        tail_lens = jnp.where(jnp.full((8, LANE), count, jnp.int32) == slot + 1, lens_tile(slot), tail_lens)
    lens_mine[...] = tail_lens

    @pl.when(d < n_dp - 1)
    def _():
        send_tok().start()
        send_lens().start()

    @pl.when(d == 0)
    def _():
        tok_b[...] = jnp.zeros_like(tok_b)
        got_cot[...] = jnp.zeros_like(got_cot)
        lens_land[...] = jnp.zeros_like(lens_land)

    @pl.when(d == n_dp - 1)
    def _():
        back_mixed[...] = jnp.zeros_like(back_mixed)
        back_grad[...] = jnp.zeros_like(back_grad)

    scan_copies = [copies.make(scan_mine.at[k], scan_land.at[k], (d + (1 << k), t)) for k in range(dp_steps)]
    scan_mine[0] = jnp.full((8, LANE), count, jnp.int32)

    def scan_start(k):
        @pl.when(d + (1 << k) < n_dp)
        def _():
            scan_copies[k]().start()

    def scan_end(k):
        scan_mine[k + 1] = scan_mine[k]

        @pl.when(d + (1 << k) < n_dp)
        def _():
            scan_copies[k]().wait_send()

        @pl.when(d >= (1 << k))
        def _():
            scan_copies[k]().wait_recv()
            scan_mine[k + 1] = scan_mine[k] + scan_land[k]

    scan_start(0)

    def gather(full, r):
        mine = full.at[r, t]
        return (
            copies.make(mine, mine, across),
            copies.make(mine, mine, core),
            copies.make(full.at[r, t ^ 2], full.at[r, t ^ 2], core),
        )

    def gather_start(link):
        link[0]().start()
        link[1]().start()

    def gather_pass(link):
        link[0]().wait_recv()
        link[2]().start()

    def gather_end(link):
        link[0]().wait_send()
        link[1]().wait()
        link[2]().wait()

    def summing(kind, r):
        return (
            copies.make(part.at[kind, r, t ^ 1], land_core.at[kind, r, 0], core),
            copies.make(part.at[kind, r, t ^ 3], land_core.at[kind, r, 1], core),
            copies.make(part.at[kind, r, t ^ 2], land_x.at[kind, r], across),
        )

    def quarter_of(i):
        return t ^ jnp.where(i == 0, 3, jnp.where(i == 3, 0, i))

    def sum_step(link, kind, r, i, q, value):
        @pl.when(i < 2)
        def _():
            part[kind, r, q] = value.astype(BF16)

        @pl.when(i == 0)
        def _():
            link[1]().start()

        @pl.when(i == 1)
        def _():
            link[0]().start()

        @pl.when(i == 2)
        def _():
            link[1]().wait_recv()
            part[kind, r, q] = (value + land_core[kind, r, 1].astype(F32)).astype(BF16)
            link[2]().start()

        @pl.when(i == 3)
        def _():
            link[0]().wait_recv()
            part[kind, r, q] = (value + land_core[kind, r, 0].astype(F32)).astype(BF16)

    def sum_all(link, kind, r, make_part):
        def run(i, _):
            q = quarter_of(i)
            sum_step(link, kind, r, i, q, make_part(q))
            return _

        lax.fori_loop(0, 4, run, None)

    def sum_end(link):
        link[0]().wait_send()
        link[1]().wait_send()
        link[2]().wait()

    def sum_total(kind, r, rows):
        return part[kind, r, t, rows].astype(F32) + land_x[kind, r, rows].astype(F32)

    link_n1 = [gather(n1, r) for r in range(2)]
    link_n2 = [gather(n2, r) for r in range(2)]
    link_cot = [gather(cot, r) for r in range(2)]
    link_gm = [gather(gm, r) for r in range(2)]

    def rows_of(q):
        return pl.ds(pl.multiple_of(q * quarter, quarter), quarter)

    def first_tokens(r, rows):
        return (tok_ref[0, rows] if r == 0 else tok_b[rows]).astype(F32)

    def first_norm(r):
        def body(rows):
            normed, _ = normalize(first_tokens(r, rows))
            n1[r, t, rows] = (normed * attn_gain + attn_shift).astype(BF16)

        over_chunks(quarter, body)

    sums[...] = jnp.zeros_like(sums)
    bias_acc[...] = jnp.zeros_like(bias_acc)

    def add_sum(row, value):
        sums[row : row + 1] = sums[row : row + 1] + jnp.sum(value, axis=0, keepdims=True)

    def load_cotangent(r):
        def body(rows):
            value = cotan_ref[0, rows].astype(F32)
            if r == 1:
                value = jnp.where(carried_wide, got_cot[rows].astype(F32), cotan_ref[1, rows].astype(F32))
            cot[r, t, rows] = value.astype(BF16)
            add_sum(5, value)

        over_chunks(quarter, body)

    first_norm(0)
    gather_start(link_n1[0])
    load_cotangent(0)

    third = 3 * HEAD_DIM
    for j in range(3):
        wc[:, j * LANE : (j + 1) * LANE] = wqkv_ref[j, :, 0:LANE]
        bc[:, j * LANE : (j + 1) * LANE] = bqkv_ref[j : j + 1, 0:LANE]
    last = [wqkv_ref[j, :, LANE:third].astype(F32) for j in range(3)]
    wc[:, 3 * LANE : 4 * LANE] = jnp.concatenate([last[0], last[1]], axis=1).astype(BF16)
    wc[:, 4 * LANE : 5 * LANE] = jnp.concatenate([last[2], jnp.zeros_like(last[2])], axis=1).astype(BF16)
    last = [bqkv_ref[j : j + 1, LANE:third] for j in range(3)]
    bc[:, 3 * LANE : 4 * LANE] = jnp.concatenate([last[0], last[1]], axis=1)
    bc[:, 4 * LANE : 5 * LANE] = jnp.concatenate([last[2], jnp.zeros_like(last[2])], axis=1)
    for h in range(3):
        woe[h * LANE : h * LANE + HEAD_DIM] = wout_ref[h * HEAD_DIM : (h + 1) * HEAD_DIM]
        woe[h * LANE + HEAD_DIM : (h + 1) * LANE] = jnp.zeros((HEAD_DIM, features), BF16)

    def ends_of(r):
        tile = lens_tile(0) if r == 0 else jnp.where(carried_tile, lens_land[...], lens_tile(1))
        first = tile[0:1]
        second = first + tile[1:2]
        return first, second, second + tile[2:3]

    def segment_of(ends, base, rows):
        place = lax.broadcasted_iota(jnp.int32, (rows, LANE), 0) + base
        return [place >= end for end in ends]

    def tables(r):
        ends = ends_of(r)
        turns = [end.astype(F32) * freq_ref[...] for end in ends]
        cosines = [jnp.cos(turn) for turn in turns]
        sines = [jnp.sin(turn) * line_ref[...] for turn in turns]

        def body(rows):
            passed = segment_of(ends, rows.start, CHUNK)
            at = pl.ds(rows.start // CHUNK, 1)
            cos_base, sin_base = base_ref[0, at], base_ref[1, at]
            cos_start = jnp.broadcast_to(cos_base, (CHUNK, LANE))
            sin_start = jnp.broadcast_to(sin_base, (CHUNK, LANE))
            for ge, cosine, sine in zip(passed, cosines, sines):
                cos_start = jnp.where(ge, cos_base * cosine + sin_base * sine, cos_start)
                sin_start = jnp.where(ge, sin_base * cosine - cos_base * sine, sin_start)
            cos_place, sin_place = rope_ref[0], rope_ref[1]
            table_c[r, rows] = cos_place * cos_start - sin_place * sin_start
            table_s[r, rows] = sin_place * cos_start + cos_place * sin_start

        over_chunks(4 * quarter, body)

    tables(0)
    scan_end(0)
    for k in range(1, dp_steps):
        scan_start(k)
        scan_end(k)
    carried_tile = (scan_mine[dp_steps] - count - d * own_rows) > 0
    carried_wide = jnp.broadcast_to(carried_tile[0:1, 0:1], (CHUNK, features))

    @pl.when(d > 0)
    def _():
        send_lens().wait_recv()
        send_tok().wait_recv()

    @pl.when(d < n_dp - 1)
    def _():
        send_lens().wait_send()
        send_tok().wait_send()
        send_cot().start()

    def pick_b(rows):
        value = jnp.where(carried_wide, tok_b[rows].astype(F32), tok_ref[1, rows].astype(F32))
        tok_b[rows] = value.astype(BF16)

    over_chunks(quarter, pick_b)
    first_norm(1)
    gather_pass(link_n1[0])
    gather_start(link_n1[1])
    tables(1)

    def project(r):
        ends = ends_of(r)

        def run(q, _):
            rows = rows_of(q)
            both = dot_nn(n1[r, q], wc[...]) + bc[...]
            lane = lanes((quarter, LANE))
            ge = segment_of(ends, q * quarter, quarter)
            gene = sum(g.astype(jnp.int32) for g in ge)
            in_mask = (lane >= MASK_AT) & (lane < TOTAL_AT)
            same = in_mask & (lane - MASK_AT == gene)
            extra_q = jnp.where(in_mask & ~same, FAR, 0.0)
            extra_k = jnp.where(same | ((lane >= TOTAL_AT) & (lane < TOTAL_AT + 3)), 1.0, 0.0)
            extra_v = jnp.where((lane >= MASK_AT) & (lane < MASK_AT + 3), 1.0, 0.0)
            cosine, sine = table_c[r, rows], table_s[r, rows]
            blocks = [both[:, j * LANE : (j + 1) * LANE] for j in range(5)]
            for h in range(3):
                query = (blocks[0], pltpu.roll(blocks[0], 64, 1), blocks[3])[h]
                key = (blocks[1], pltpu.roll(blocks[1], 64, 1), pltpu.roll(blocks[3], 64, 1))[h]
                value = (blocks[2], pltpu.roll(blocks[2], 64, 1), blocks[4])[h]
                query = (query * cosine + swap_halves(query) * sine) * HEAD_DIM**-0.5 + extra_q
                key = key * cosine + swap_halves(key) * sine + extra_k
                value = jnp.where(lane < HEAD_DIM, value, extra_v)
                heads_q[r, h, rows] = query.astype(BF16)
                heads_k[r, h, rows] = key.astype(BF16)
                heads_v[r, h, rows] = value.astype(BF16)
            return _

        lax.fori_loop(0, 4, run, None)

    def attend(r):
        def run(i, _):
            h, q = i // 4, i % 4
            rows = rows_of(q)
            query = heads_q[r, h, rows]
            scores = dot_nt(query, heads_k[r, h])
            top = jnp.max(scores, -1, keepdims=True)
            probs = jnp.exp(scores - top).astype(BF16)
            mixed_values = dot_nn(probs, heads_v[r, h])
            lane = lanes((quarter, LANE))
            total = mixed_values[:, MASK_AT : MASK_AT + 1]
            out = mixed_values * (1.0 / total)
            head_out[r, h, rows] = jnp.where(lane < HEAD_DIM, out, 0.0).astype(BF16)
            parts = three_parts(-(top + jnp.log(total)))
            query = query.astype(F32)
            for at, value in enumerate(parts):
                query = jnp.where(lane == TOTAL_AT + at, value, query)
            heads_q[r, h, rows] = query.astype(BF16)
            return _

        lax.fori_loop(0, 12, run, None)

    def close_attention(r, link):
        def make(q):
            rows = rows_of(q)
            joined = jnp.concatenate([head_out[r, h, rows] for h in range(3)], axis=1)
            return dot_nn(joined, woe[...])

        sum_all(link, 0, r, make)

    def second_norm(r):
        def body(rows):
            middle = first_tokens(r, rows) + sum_total(0, r, rows) + out_bias
            mid[r, rows] = middle
            normed, _ = normalize(middle)
            n2[r, t, rows] = (normed * ffn_gain + ffn_shift).astype(BF16)

        over_chunks(quarter, body)

    def feed(r, link):
        def make(q):
            hidden = dot_nn(n2[r, q], wup_ref[...]) + bup_ref[...]
            below = 0.5 * (1.0 + lax.erf(hidden * 0.5**0.5))
            density = jnp.exp(hidden * hidden * -0.5) * (2.0 * np.pi) ** -0.5
            act[r, rows_of(q)] = (hidden * below).astype(BF16)
            grad = dot_nt(cot[r, q], wdown_ref[...]) * (below + hidden * density)
            add_sum(6, grad)
            low = grad.astype(BF16)
            slope[r, q] = low
            return dot_nt(low, wup_ref[...])

        sum_all(link, 0, r, make)

    def close_feed(r, link):
        sum_all(link, 1, r, lambda q: dot_nn(act[r, rows_of(q)], wdown_ref[...]))

    def finish_mixed(r):
        def body(rows):
            mixed[r, rows] = (mid[r, rows] + sum_total(1, r, rows) + down_bias).astype(BF16)

        over_chunks(quarter, body)

    def back_second_norm(r):
        def body(rows):
            incoming = sum_total(0, r, rows)
            normed, inv_std = normalize(mid[r, rows])
            grad = cot[r, t, rows].astype(F32) + norm_back(incoming, normed, inv_std, ffn_gain)
            gmid[r, rows] = grad
            gm[r, t, rows] = grad.astype(BF16)
            add_sum(3, incoming * normed)
            add_sum(4, incoming)
            add_sum(2, grad)

        over_chunks(quarter, body)

    def open_heads(r):
        def run(q, _):
            rows = rows_of(q)
            grads = dot_nt(gm[r, q], woe[...])
            lane = lanes((quarter, LANE))
            for h in range(3):
                low = grads[:, h * LANE : (h + 1) * LANE].astype(BF16).astype(F32)
                dots = jnp.sum(low * head_out[r, h, rows].astype(F32), -1, keepdims=True)
                for at, value in enumerate(three_parts(-dots)):
                    low = jnp.where(lane == MASK_AT + at, value, low)
                head_grad[h, rows] = low.astype(BF16)
            return _

        lax.fori_loop(0, 4, run, None)

    def unrotate(r, rows, value):
        return value * table_c[r, rows] - swap_halves(value) * table_s[r, rows]

    def put(r, j, h, rows, value):
        at = h * 3 + j
        bias_acc[pl.ds(at, 1)] = bias_acc[pl.ds(at, 1)] + jnp.sum(value, axis=0, keepdims=True)
        block = slice(j * LANE, (j + 1) * LANE)
        tail = slice(3 * LANE, 4 * LANE) if j < 2 else slice(4 * LANE, 5 * LANE)

        @pl.when(h == 0)
        def _():
            dp_low[r, rows, block] = value.astype(BF16)

        @pl.when(h == 1)
        def _():
            first = dp_low[r, rows, block].astype(F32)
            dp_low[r, rows, block] = (first + pltpu.roll(value, 64, 1)).astype(BF16)

        @pl.when(h == 2)
        def _():
            if j == 0:
                other = dp_low[r, rows, tail].astype(F32)
                dp_low[r, rows, tail] = (other + value).astype(BF16)
            else:
                moved = pltpu.roll(value, 64, 1) if j == 1 else value
                dp_low[r, rows, tail] = moved.astype(BF16)

    def attend_back(r, h):
        dq_acc[...] = jnp.zeros_like(dq_acc)

        def run(b, _):
            rows = rows_of(b)
            keys = heads_k[r, h, rows]
            lane = lanes((quarter, LANE))
            probs = jnp.exp(dot_nt(keys, heads_q[r, h]))
            grads = probs * dot_nt(heads_v[r, h, rows], head_grad[h])
            low = grads.astype(BF16)
            dv = dot_nn(probs.astype(BF16), head_grad[h])
            put(r, 2, h, rows, jnp.where(lane < HEAD_DIM, dv, 0.0))
            dk = dot_nn(low, heads_q[r, h])
            put(r, 1, h, rows, unrotate(r, rows, jnp.where(lane < HEAD_DIM, dk, 0.0)))
            dq_acc[...] += dot_tn(low, keys)
            return _

        lax.fori_loop(0, 4, run, None)

        def close(q, _):
            rows = rows_of(q)
            lane = lanes((quarter, LANE))
            dq = jnp.where(lane < HEAD_DIM, dq_acc[rows], 0.0) * HEAD_DIM**-0.5
            put(r, 0, h, rows, unrotate(r, rows, dq))
            return _

        lax.fori_loop(0, 4, close, None)

    def close_back(r, link):
        def make(q):
            rows = rows_of(q)
            return dot_nt(dp_low[r, rows], wc[...])

        sum_all(link, 0, r, make)

    def back_first_norm(r):
        def body(rows):
            incoming = sum_total(0, r, rows)
            normed, inv_std = normalize(first_tokens(r, rows))
            grad = gmid[r, rows] + norm_back(incoming, normed, inv_std, attn_gain)
            ingrad[r, rows] = grad.astype(BF16)
            add_sum(0, incoming * normed)
            add_sum(1, incoming)

        over_chunks(quarter, body)

    def flat(ref, r, at):
        here = pl.ds(pl.multiple_of(at, LANE), 256)
        return ref[r, :, here] if ref is act else ref[r, :, :, here].reshape(4 * quarter, 256)

    def weight_grad(left, right, target):
        def run(i, _):
            total = sum(dot_tn(flat(left, r, i * 256), right[r].reshape(4 * quarter, features)) for r in range(2))
            target[pl.ds(pl.multiple_of(i * 256, 256), 256)] = total.astype(BF16)
            return _

        lax.fori_loop(0, features // 256, run, None)

    def up_grad():
        weight_grad(n2, slope, gup)

    def down_grad():
        weight_grad(act, cot, gdown)

    def out_grad():
        for h in range(3):
            total = sum(dot_tn(head_out[r, h], gm[r].reshape(4 * quarter, features)) for r in range(2))
            gout[h * HEAD_DIM : (h + 1) * HEAD_DIM] = total[0:HEAD_DIM].astype(BF16)

    def qkv_grad():
        def run(i, _):
            total = sum(dot_tn(flat(n1, r, i * 256), dp_low[r]) for r in range(2))
            gqkv[pl.ds(pl.multiple_of(i * 256, 256), 256)] = total.astype(BF16)
            return _

        lax.fori_loop(0, features // 256, run, None)

    order = tuple(range(dp_steps))
    turned = (order[1], order[0]) + order[2:] if dp_steps > 1 else order
    red_down = Reduce(copies, gdown, land_down, gdown_out, out_sems.at[2], features, order, d, t)
    red_up = Reduce(copies, gup, land_up, gup_out, out_sems.at[3], features, turned, d, t)
    red_out = Reduce(copies, gout, land_out, gout_out, out_sems.at[4], 3 * HEAD_DIM, order, d, t)
    red_qkv = Reduce(copies, gqkv, land_qkv, gqkv_out, out_sems.at[5], features, order, d, t)

    gather_end(link_n1[0])
    project(0)
    gather_start(link_cot[0])
    attend(0)
    link_o0 = summing(0, 0)
    close_attention(0, link_o0)
    gather_pass(link_n1[1])
    gather_end(link_n1[1])
    project(1)
    sum_end(link_o0)
    second_norm(0)
    gather_start(link_n2[0])

    @pl.when(d > 0)
    def _():
        send_cot().wait_recv()

    @pl.when(d < n_dp - 1)
    def _():
        send_cot().wait_send()

    load_cotangent(1)
    gather_pass(link_cot[0])
    attend(1)
    gather_pass(link_n2[0])
    gather_start(link_cot[1])
    link_o1 = summing(0, 1)
    close_attention(1, link_o1)
    gather_end(link_n2[0])
    gather_end(link_cot[0])
    link_g0 = summing(0, 0)
    feed(0, link_g0)
    sum_end(link_o1)
    second_norm(1)
    gather_start(link_n2[1])
    link_m0 = summing(1, 0)
    close_feed(0, link_m0)
    gather_pass(link_cot[1])
    sum_end(link_g0)
    back_second_norm(0)
    gather_start(link_gm[0])
    gather_pass(link_n2[1])
    gather_end(link_cot[1])
    gather_end(link_n2[1])
    link_g1 = summing(0, 1)
    feed(1, link_g1)
    gather_pass(link_gm[0])
    down_grad()
    red_down.start()
    up_grad()
    red_up.start()
    link_m1 = summing(1, 1)
    close_feed(1, link_m1)
    gather_end(link_gm[0])
    open_heads(0)
    attend_back(0, 0)
    sum_end(link_g1)
    back_second_norm(1)
    gather_start(link_gm[1])
    red_down.tick()
    red_up.tick()
    attend_back(0, 1)
    red_down.tick()
    red_up.tick()
    attend_back(0, 2)
    link_f0 = summing(0, 0)
    close_back(0, link_f0)
    gather_pass(link_gm[1])
    sum_end(link_m0)
    finish_mixed(0)
    sum_end(link_m1)
    finish_mixed(1)
    return_mixed = copies.make(mixed.at[1], back_mixed, before)
    return_grad = copies.make(ingrad.at[1], back_grad, before)

    @pl.when(d > 0)
    def _():
        return_mixed().start()

    gather_end(link_gm[1])
    out_grad()
    red_out.start()
    open_heads(1)
    red_down.tick()
    red_up.tick()
    attend_back(1, 0)
    red_down.tick()
    red_up.tick()
    red_out.tick()
    sum_end(link_f0)
    back_first_norm(0)
    attend_back(1, 1)
    red_down.tick()
    red_up.tick()
    red_out.tick()
    attend_back(1, 2)
    link_f1 = summing(0, 1)
    close_back(1, link_f1)
    qkv_grad()
    red_qkv.start()
    while red_down.left() or red_up.left() or red_out.left():
        red_down.tick()
        red_up.tick()
        red_out.tick()
    sum_end(link_f1)
    back_first_norm(1)

    @pl.when(d > 0)
    def _():
        return_grad().start()

    acc = [[bias_acc[h * 3 + j : h * 3 + j + 1] for j in range(3)] for h in range(3)]
    for j in range(3):
        sums[7:8, j * LANE : (j + 1) * LANE] = acc[0][j] + pltpu.roll(acc[1][j], 64, 1)
    sums[7:8, 3 * LANE : 4 * LANE] = acc[2][0] + pltpu.roll(acc[2][1], 64, 1)
    sums[7:8, 4 * LANE : 5 * LANE] = acc[2][2]
    partners = [core, across] + [(d ^ (1 << k), t) for k in range(dp_steps)]
    shared = lax.broadcasted_iota(jnp.int32, (8, features), 0) < 6
    for k, partner in enumerate(partners):
        copy = copies.make(sums, sums_land.at[k], partner)
        copy().start()
        copy().wait()
        extra = sums_land[k]
        sums[...] = sums[...] + (jnp.where(shared, extra, 0.0) if k < 2 else extra)
        red_qkv.tick()

    @pl.when(d > 0)
    def _():
        return_mixed().wait_send()
        return_grad().wait_send()

    @pl.when(d < n_dp - 1)
    def _():
        return_mixed().wait_recv()
        return_grad().wait_recv()

    def settle(rows):
        for own, back in ((mixed, back_mixed), (ingrad, back_grad)):
            mine, returned = own[1, rows].astype(F32), back[rows].astype(F32)
            middle = jnp.where(carried_wide, returned, mine)
            own[1, rows] = jnp.where(count_wide >= 2, middle, 0.0).astype(BF16)
            own[2, rows] = jnp.where(count_wide >= 3, returned, 0.0).astype(BF16)

    over_chunks(quarter, settle)
    store_mixed = pltpu.make_async_copy(mixed, mixed_out, out_sems.at[0])
    store_grad = pltpu.make_async_copy(ingrad, grad_out, out_sems.at[1])
    store_mixed.start()
    store_grad.start()
    total = jnp.zeros((1, head_ref.shape[1]), F32)
    for slot in range(slots):
        logits = dot_nn(mixed[slot], head_ref[...])
        raised = jnp.exp(logits - jnp.max(logits, -1, keepdims=True))
        probs = raised / jnp.sum(raised, -1, keepdims=True)
        one = jnp.sum(probs, axis=0, keepdims=True)
        total = total + jnp.where(jnp.full(one.shape, count, jnp.int32) > slot, one, 0.0)
    codon_out[...] = total
    small_out[...] = sums[...]
    while red_qkv.left():
        red_qkv.tick()
    store_mixed.wait()
    store_grad.wait()


def body(
    tokens,
    cotangent,
    lengths,
    row_counts,
    attn_gain,
    attn_shift,
    qkv_weight,
    qkv_bias,
    out_weight,
    out_bias,
    ffn_gain,
    ffn_shift,
    up_weight,
    up_bias,
    down_weight,
    down_bias,
    head_weight,
    codon_freq,
):
    slots, quarter, features = tokens.shape
    n_dp = lax.axis_size("dp")
    steps = n_dp.bit_length() - 1
    length = 4 * quarter
    half = HEAD_DIM // 2
    freqs = np.float32(BASE) ** (-np.arange(half, dtype=np.float32) / np.float32(half))
    freq_lane = np.tile(freqs.astype(np.float32), LANE // half)
    sign = np.concatenate([-np.ones(half), np.ones(half), np.zeros(HEAD_DIM)]).astype(np.float32)

    def turned(places):
        angles = places[:, None].astype(np.float64) * freq_lane[None].astype(np.float64)
        return np.stack([np.cos(angles) * np.abs(sign), np.sin(angles) * sign]).astype(np.float32)

    rope, bases = turned(np.arange(CHUNK)), turned(np.arange(0, length, CHUNK))
    vectors = jnp.stack([attn_gain, attn_shift, out_bias, ffn_gain, ffn_shift, down_bias, down_bias, down_bias])
    vmem, smem = pl.BlockSpec(memory_space=pltpu.VMEM), pl.BlockSpec(memory_space=pltpu.SMEM)
    anywhere = pl.BlockSpec(memory_space=pl.ANY)
    wide = (quarter, features)

    def low(*shape):
        return pltpu.VMEM(shape, BF16)

    def full(*shape):
        return pltpu.VMEM(shape, F32)

    out_width = 3 * HEAD_DIM
    n_sems = 24 + 24 + 3 + steps + 2 + 4 * 2 * steps + 2 + steps
    scratch = [
        low(2, 4, *wide),
        low(2, 4, *wide),
        low(2, 4, *wide),
        low(2, 4, *wide),
        low(2, 3, length, LANE),
        low(2, 3, length, LANE),
        low(2, 3, length, LANE),
        low(2, 3, length, LANE),
        low(3, length, LANE),
        full(length, LANE),
        low(2, length, 5 * LANE),
        low(2, length, features),
        low(2, 4, *wide),
        low(2, 2, 4, *wide),
        low(2, 2, 2, *wide),
        low(2, 2, *wide),
        full(2, *wide),
        full(2, *wide),
        full(2, length, LANE),
        full(2, length, LANE),
        low(features, 5 * LANE),
        full(1, 5 * LANE),
        low(3 * LANE, features),
        low(*wide),
        low(*wide),
        pltpu.VMEM((steps + 1, 8, LANE), jnp.int32),
        pltpu.VMEM((steps, 8, LANE), jnp.int32),
        pltpu.VMEM((8, LANE), jnp.int32),
        pltpu.VMEM((8, LANE), jnp.int32),
        low(features, features),
        low(features, features),
        low(out_width, features),
        low(features, 5 * LANE),
        low(Reduce.land_rows(features, steps), features),
        low(Reduce.land_rows(features, steps), features),
        low(*wide),
        low(*wide),
        full(8, features),
        full(2 + steps, 8, features),
        full(16, LANE),
        pltpu.SemaphoreType.DMA((n_sems,)),
        pltpu.SemaphoreType.DMA((n_sems,)),
        pltpu.SemaphoreType.DMA((6,)),
    ]
    outs = pl.pallas_call(
        functools.partial(layer_kernel, n_dp, slots, quarter, features),
        out_shape=(
            jax.ShapeDtypeStruct(tokens.shape, BF16),
            jax.ShapeDtypeStruct(tokens.shape, BF16),
            jax.ShapeDtypeStruct((features, features), BF16),
            jax.ShapeDtypeStruct((features, features), BF16),
            jax.ShapeDtypeStruct((out_width, features), BF16),
            jax.ShapeDtypeStruct((features, 5 * LANE), BF16),
            jax.ShapeDtypeStruct((8, features), F32),
            jax.ShapeDtypeStruct((1, head_weight.shape[1]), F32),
        ),
        in_specs=[smem, smem] + [vmem] * 14,
        out_specs=(anywhere,) * 6 + (vmem, vmem),
        scratch_shapes=scratch,
        compiler_params=pltpu.CompilerParams(
            collective_id=0, has_side_effects=True, vmem_limit_bytes=64 * 1024 * 1024
        ),
    )(
        row_counts,
        lengths,
        tokens,
        cotangent,
        qkv_weight,
        qkv_bias,
        out_weight,
        up_weight,
        down_weight,
        up_bias[None],
        vectors,
        head_weight,
        jnp.asarray(freq_lane[None]),
        jnp.asarray(rope),
        jnp.asarray(bases),
        jnp.asarray(sign[None]),
    )
    mixed, input_grad, gdown, gup, gout, gqkv, small, codon = outs
    mean_prob = codon / (row_counts[0] * quarter).astype(F32)
    codon_gap = (jnp.log(mean_prob) - jnp.log(codon_freq)).reshape(1, 1, -1)

    def spread(packed):
        pairs = packed[..., : 3 * LANE].reshape(packed.shape[:-1] + (3, LANE))
        rest = packed[..., 3 * LANE : 3 * LANE + 3 * HEAD_DIM].reshape(packed.shape[:-1] + (3, HEAD_DIM))
        return jnp.moveaxis(jnp.concatenate([pairs, rest], axis=-1), -2, 0)

    return (
        mixed,
        input_grad,
        small[0],
        small[1],
        spread(gqkv).astype(F32),
        spread(small[7, : 5 * LANE]),
        gout.astype(F32),
        small[2],
        small[3],
        small[4],
        gup.astype(F32),
        small[6],
        gdown.astype(F32),
        small[5],
        codon_gap,
    )


def solution(mesh):
    placed = (
        P("dp", "tensor", None),
        P("dp", "tensor", None),
        P("dp", None),
        P("dp"),
        P(),
        P(),
        P(None, None, "tensor"),
        P(None, "tensor"),
        P("tensor", None),
        P(),
        P(),
        P(),
        P(None, "tensor"),
        P("tensor"),
        P("tensor", None),
        P(),
        P(),
        P(),
    )
    return jax.shard_map(
        body,
        mesh=mesh,
        in_specs=placed,
        out_specs=(
            P("dp", "tensor", None),
            P("dp", "tensor", None),
            P(),
            P(),
            P(None, None, "tensor"),
            P(None, "tensor"),
            P("tensor", None),
            P(),
            P(),
            P(),
            P(None, "tensor"),
            P("tensor"),
            P("tensor", None),
            P(),
            P("dp", "tensor", None),
        ),
        check_vma=False,
    )
```

time: 739 us -> 272 us (0.37); the launches traced: 728 us -> 272 us
  waiting for transfers between devices: 340 us -> 0 us
  Pallas kernels: 0 us -> 252 us
  matrix products: 119 us -> 0 us
  blocking collectives: 113 us -> 0 us
  other arithmetic: 79.9 us -> 6.48 us
  local copies, waits for them, and re-layouts: 36 us -> 12 us
  starting transfers between devices: 18 us -> 0 us
  between operations: 15.9 us -> 1.54 us
    pallas_call x0 -> x1, Pallas kernels: none -> 252 us  [body(): pl.pallas_call(functools.partial(layer_kernel, n_dp, slots, quarter, feat...]
    psum x1 -> x0, waiting for transfers between devices: 139 us -> none  [run_layer(): lax.psum((qkv_weight_grad, qkv_bias_grad, out_weight_grad, up_weight_grad...]
    reduce_scatter x4 -> x0, waiting for transfers between devices: 126 us -> none  [the longest x2 74.5 us: narrow_sums(): lax.psum_scatter(value.astype(jnp.bfloat16), 'tensor', scatter_dimension=...]
    dot_general x26 -> x0, matrix products: 118 us -> none  [the longest x4 15.8 us: masked_scores(): jnp.einsum('qhe,khe->hqk', queries, keys, preferred_element_type=jnp.floa...]
    psum x2 -> x0, blocking collectives: 101 us -> none  [the longest x1 59.1 us: run_layer(): lax.psum((qkv_weight_grad, qkv_bias_grad, out_weight_grad, up_weight_grad...]
    all_gather x4 -> x0, waiting for transfers between devices: 66.8 us -> none  [the longest x2 34.4 us: spread_grads(): return lax.all_gather(value, 'tensor', axis=1, tiled=True)]
    convert_element_type x9 -> x4, other arithmetic: 38.6 us -> 5.36 us  [the longest x1 1.58 us: body(): gup.astype(F32)]
    reduce_sum x11 -> x0, other arithmetic: 26.4 us -> none  [the longest x2 14.8 us: attend_row(): row_total = jnp.sum(weights_raw, -1, keepdims=True)]
  transfers between devices with their start and end apart: 14 -> 0, of which waited for: 11 -> 0; matrix products, arithmetic and copies ran while one was open for 10% -> 0% of each run, Pallas kernels for 0% -> 0%
where the time goes in v1:
time: 272 us
  Pallas kernels  252 us (93%)
  local copies, waits for them, and re-layouts  12 us (4%)
  other arithmetic  6.48 us (2%)
    pallas_call x1, Pallas kernels, body(): pl.pallas_call(functools.partial(layer_kernel, n_dp, slots, quarter, feat...  252 us
    unnamed x36, local copies, waits for them, and re-layouts  6.05 us

profile of v1, /device:TPU:0, one launch (start us, length us, event | category | flops | bytes accessed | tf_op | source)
XLA Modules:
  0.0 272.0 jit_solution(17629426086038183259)
XLA Ops:
  0.6 0.0 copy-start.5
  1.3 0.0 copy-start.7
  1.3 0.0 copy-start.8
  1.4 0.0 copy-start.9
  1.4 0.0 copy-start.10
  1.4 0.0 copy-start.11
  1.4 0.0 copy-start.12
  1.4 0.0 copy-start.13
  1.4 2.4 copy.41.wqkv_ref
  3.8 0.0 copy-done.5
  3.8 0.8 copy.42.head_ref
  4.6 0.0 copy-done.7
  4.6 0.0 copy-done.8
  4.6 0.0 copy-done.9
  4.6 0.0 copy-done.10
  4.7 0.0 copy-done.11
  4.7 0.0 copy-done.12
  4.7 0.7 stack.29.vec_ref
  5.4 0.0 copy-done.13
  5.4 0.6 broadcast_in_dim.6.bup_ref
  5.9 251.9 %shard_map.325 = (bf16[3,256,768]{2,1,0:T(8,128)(2,1)}, bf16[3,256,768]{2,1,0:T(8,128)(2,1)}, bf16[768,768]{1,0:T(8,128)(2,1)}, bf16[768,768]{1,0:T(8,128)(2,1)}...) custom-call(s32[1]{0:T(128)S(6)} %copy.47.count_ref, ...), custom_call_target="tpu_custom_call" | custom-call | tf_op jit(solution)/shard_map/pallas_call | solution.py:1000
  257.9 0.7 slice_reduce_fusion.8
  258.6 0.1 reshape.55
  258.7 0.7 slice_reduce_fusion.7
  259.4 0.6 pad_maximum_fusion
  260.0 1.1 slice.40
  261.1 0.3 copy.43
  261.4 1.0 slice.41
  262.4 0.2 copy.44
  262.6 0.0 copy-start.6
  262.6 0.0 copy-start.14
  262.6 0.0 copy-start.15
  262.6 0.0 copy-start.1
  262.6 1.4 convert_bitcast_fusion
  264.0 0.0 copy-done.6
  264.0 0.7 slice_reduce_fusion
  264.6 0.0 copy-done.14
  264.6 0.0 copy-done.15
  264.6 0.5 fusion
  265.1 0.0 copy-done.1
  265.2 1.6 convert_element_type.24
  266.7 0.1 copy-done
  266.8 1.6 convert_element_type.25
  268.4 0.0 copy-done.4
  268.4 0.9 convert_element_type.23
  269.3 1.0 copy.48
  270.3 0.7 copy-done.2
  271.0 1.0 copy.49
  (11 shorter events, 0.0 us)
Async XLA Ops:
  0.6 3.1 %copy-start.5 = (bf16[768,70]{0,1:T(8,128)(2,1)S(1)}, bf16[768,70]{0,1:T(8,128)(2,1)}, u32[]{:S(2)}) copy-start(bf16[768,70]{0,1:T(8,128)(2,1)} %param.38) | copy-start | bytes 322564
  1.3 3.3 %copy-start.7 = (f32[768]{0:T(1024)S(1)}, f32[768]{0:T(1024)}, u32[]{:S(2)}) copy-start(f32[768]{0:T(1024)} %param.26) | copy-start | bytes 9220
  1.3 3.3 %copy-start.8 = (f32[768]{0:T(1024)S(1)}, f32[768]{0:T(1024)}, u32[]{:S(2)}) copy-start(f32[768]{0:T(1024)} %param.27) | copy-start | bytes 9220
  1.4 3.3 %copy-start.9 = (f32[768]{0:T(1024)S(1)}, f32[768]{0:T(1024)}, u32[]{:S(2)}) copy-start(f32[768]{0:T(1024)} %param.31) | copy-start | bytes 9220
  1.4 3.3 %copy-start.10 = (f32[768]{0:T(1024)S(1)}, f32[768]{0:T(1024)}, u32[]{:S(2)}) copy-start(f32[768]{0:T(1024)} %param.32) | copy-start | bytes 9220
  1.4 3.3 %copy-start.11 = (f32[768]{0:T(1024)S(1)}, f32[768]{0:T(1024)}, u32[]{:S(2)}) copy-start(f32[768]{0:T(1024)} %param.33) | copy-start | bytes 9220
  1.4 3.3 %copy-start.12 = (f32[768]{0:T(1024)S(1)}, f32[768]{0:T(1024)}, u32[]{:S(2)}) copy-start(f32[768]{0:T(1024)} %param.37) | copy-start | bytes 9220
  1.4 4.0 %copy-start.13 = (f32[768]{0:T(1024)S(1)}, f32[768]{0:T(1024)}, u32[]{:S(2)}) copy-start(f32[768]{0:T(1024)} %param.35) | copy-start | bytes 9220
  262.6 1.4 copy-start.6
  262.6 2.0 copy-start.14
  262.6 2.0 copy-start.15
  262.6 2.6 copy-start.1
  265.2 1.7 copy-start
  266.8 1.6 copy-start.4
  266.8 2.4 copy-start.3
  269.3 1.7 copy-start.2
